TPU v7x, 256 devices: a whole 4x4x8 slice. The times are simulated.
256 devices in a mesh: seq: 128 (over x, y, z), head: 2 (over core).
Axes of the slice: x: 4, y: 4, z: 8, core: 2. Of those that a mesh axis runs over, the one named last changes fastest.
Arguments:
- tokens: bfloat16 [65536, 1024], P('seq', 'head'), may hold values from -16 to 16
- w_qk: bfloat16 [1024, 2, 1024], P(None, None, 'head'), may hold values from -0.1875 to 0.1875
- w_value: bfloat16 [1024, 1024], P(None, 'head'), may hold values from -0.75 to 0.75
- span_start: int32 [512], P('seq'), may hold values from 0 to 65408, as said below
- span_end: int32 [512], P('seq'), may hold values from 128 to 65536, as said below
Outputs:
- attended: bfloat16 [65536, 1024], P('seq', 'head')
Inputs may be any that keep to these rules, and one draw needn't show every extreme that they name: span_start[b] is at least (b - 1) * 128 and at most b * 128, never below 0; the last block's span starts at its own first token. span_end[b] is at least (b + 1) * 128 and at most (b + 2) * 128, never above 65536; the first block's span ends at its own last token plus one.
All inputs are finite; a program needn't handle non-finite values.
Results may differ from a plain program's by a relative error of at most 0.0029.
The roundings to bfloat16 on the way count: a program that leaves them out, or rounds other values in their place, can miss the bound.
Values may be sent and summed in bfloat16 or wider, within the bound.
A program may use at most 64 MiB of HBM per device.

v0:
```python
import functools
import math

import jax
import jax.numpy as jnp
from jax import lax
from jax.experimental import pallas as pl
from jax.experimental.pallas import tpu as pltpu
from jax.sharding import PartitionSpec as P

HD = 128
B = 128
LEVELS = 6
MESH = pl.DeviceIdType.MESH
BF = jnp.bfloat16
F32 = jnp.float32
UNIT = math.log2(math.e) / math.sqrt(HD)


def reversed_bits(x, bits=7):
    out = jnp.zeros_like(x)
    for i in range(bits):
        out = out + (((x >> i) & 1) << (bits - 1 - i))
    return out


def dot(a, b):
    return jnp.dot(a, b, preferred_element_type=F32)


def pool_halves(x, blocks):
    rows, cols = x.shape
    y = x.reshape(blocks, 2, rows // (2 * blocks), cols)
    y = (y[:, 0] + y[:, 1]) * 0.5
    return y.reshape(rows // 2, cols).astype(BF)


def twice(x, blocks):
    rows, cols = x.shape
    y = x.reshape(blocks, rows // blocks, cols)
    return jnp.concatenate([y, y], axis=1).reshape(2 * rows, cols)


def attend(q, k, v, bias=None):
    s = lax.dot_general(q, k, (((1,), (1,)), ((), ())), preferred_element_type=F32)
    if bias is not None:
        s = s + bias
    top = jnp.max(s, axis=-1, keepdims=True)
    w = jnp.exp2((s - top) * UNIT)
    return top * UNIT, jnp.sum(w, axis=-1, keepdims=True), dot(w.astype(BF), v)


def merge(a, b):
    top = jnp.maximum(a[0], b[0])
    ka, kb = jnp.exp2(a[0] - top), jnp.exp2(b[0] - top)
    return top, a[1] * ka + b[1] * kb, a[2] * ka + b[2] * kb


def group(level):
    return 1 << (level - 2)


def siblings(me, level):
    g = group(level)
    own = me // g
    base = (own + 1 - 2 * (own % 2)) * g
    return [base + (me + k) % g for k in range(g)]


def kernel(
    count,
    tok_hbm, wqk_hbm, wv_hbm, start_ref, end_ref,
    out_ref,
    tok_raw, tokp, wqk, wv, wq_s, wk_s, acc,
    q0, k0, v0, q1, k1, v1, q2, q3, q4, q5, q6,
    s2, s3, s4, s5, s6,
    r2, r3, r4, r5, r6,
    fpeak, ftot, fnum,
    load_sem, send_sem, recv_sem,
):
    me, core = lax.axis_index("seq"), lax.axis_index("head")
    heads = q0.shape[0]
    sends = {2: s2, 3: s3, 4: s4, 5: s5, 6: s6}
    lands = {2: r2, 3: r3, 4: r4, 5: r5, 6: r6}

    loads = [
        pltpu.make_async_copy(tok_hbm, tok_raw, load_sem.at[0]),
        pltpu.make_async_copy(wqk_hbm, wqk, load_sem.at[1]),
        pltpu.make_async_copy(wv_hbm, wv, load_sem.at[2]),
    ]
    for load in loads:
        load.start()

    right, left = (me + 1) % count, (me + count - 1) % count
    twin = (me, 1 - core)
    greet = [twin, (right, core), (left, core)]
    for level in range(2, LEVELS + 1):
        greet += [(p, core) for p in siblings(me, level)]
    barrier = pltpu.get_barrier_semaphore()
    for device in greet:
        pl.semaphore_signal(barrier, inc=1, device_id=device, device_id_type=MESH)

    row = lax.broadcasted_iota(jnp.int32, (B, B), 0)
    col = lax.broadcasted_iota(jnp.int32, (B, B), 1)
    perm = jnp.where(reversed_bits(row) == col, 1.0, 0.0).astype(BF)

    loads[0].wait()
    for b in range(4):
        tokp[core, b + 1] = dot(perm, tok_raw[b * B : (b + 1) * B]).astype(BF)

    pl.semaphore_wait(barrier, len(greet))

    def send(src, dst, sem, device):
        copy = pltpu.make_async_remote_copy(
            src_ref=src, dst_ref=dst, send_sem=send_sem.at[sem], recv_sem=recv_sem.at[sem],
            device_id=device, device_id_type=MESH,
        )
        copy.start()
        return copy

    swap = send(tokp.at[core, pl.ds(1, 4)], tokp.at[core, pl.ds(1, 4)], 0, twin)
    to_right = send(tokp.at[core, 4], tokp.at[core, 0], 1, (right, core))
    to_left = send(tokp.at[core, 1], tokp.at[core, 5], 7, (left, core))

    loads[1].wait()
    wq_s[...] = wqk[:, 0, :]
    wk_s[...] = wqk[:, 1, :]
    loads[2].wait()

    half = pl.multiple_of(core * 512, 512)
    other = pl.multiple_of((1 - core) * 512, 512)
    weights = (wk_s, wv, wq_s)
    mine = tokp[core, 1:5].reshape(4 * B, 512)
    for i, w in enumerate(weights):
        acc[i] = dot(mine, w[pl.ds(half, 512), :])

    swap.wait()
    theirs = tokp[1 - core, 1:5].reshape(4 * B, 512)

    quarter_row = lax.broadcasted_iota(jnp.int32, (32, 32), 0)
    quarter_col = lax.broadcasted_iota(jnp.int32, (32, 32), 1)

    def mix(rows, apart):
        r, c = quarter_row[:rows], quarter_col[:rows]
        return jnp.where((c == r) | (c == (r ^ apart)), 0.5, 0.0).astype(BF)

    def narrow():
        r = lax.broadcasted_iota(jnp.int32, (16, 32), 0)
        c = lax.broadcasted_iota(jnp.int32, (16, 32), 1)
        first = (r // 4) * 8 + r % 4
        five = jnp.where((c == first) | (c == first + 4), 0.5, 0.0).astype(BF)
        r = lax.broadcasted_iota(jnp.int32, (8, 16), 0)
        c = lax.broadcasted_iota(jnp.int32, (8, 16), 1)
        first = (r // 2) * 4 + r % 2
        six = jnp.where((c == first) | (c == first + 2), 0.5, 0.0).astype(BF)
        return five, six

    five, six = narrow()
    last = {}
    for i in range(2):
        full = (acc[i] + dot(theirs, weights[i][pl.ds(other, 512), :])).astype(BF)
        x = full.astype(F32)
        store0, store1 = (k0, k1) if i == 0 else (v0, v1)
        for h in range(heads):
            cols = slice(h * HD, (h + 1) * HD)
            store0[h, B : 5 * B] = full[:, cols]
        l1 = pool_halves(x, 4)
        l2 = pool_halves(l1.astype(F32), 4)
        l3 = pool_halves(l2.astype(F32), 4)
        l4 = pool_halves(l3.astype(F32), 4)
        l5 = dot(five, l4).astype(BF)
        l6 = dot(six, l5)
        for h in range(heads):
            cols = slice(h * HD, (h + 1) * HD)
            store1[h] = l1[:, cols]
            s2[h, i] = l2[:, cols]
            s3[h, i] = l3[:, cols]
            s4[h, i] = l4[:, cols]
            s5[h, i] = l5[:, cols]
        last[i] = l6
    both = jnp.concatenate([last[0], last[1]], axis=0).astype(BF)
    for h in range(heads):
        s6[h] = both[:, h * HD : (h + 1) * HD]

    send(s2, r2, 2, (siblings(me, 2)[0], core))
    for level in range(3, LEVELS + 1):
        for p in siblings(me, level):
            send(sends[level], lands[level].at[me % group(level)], level, (p, core))

    full = (acc[2] + dot(theirs, wq_s[pl.ds(other, 512), :])).astype(BF)
    l1 = pool_halves(full.astype(F32), 4)
    l2 = pool_halves(l1.astype(F32), 4)
    l3 = pool_halves(l2.astype(F32), 4)
    l4 = pool_halves(l3.astype(F32), 4)
    l5 = dot(mix(32, 4), l4).astype(BF)
    l6 = dot(mix(32, 2), l5).astype(BF)
    for h in range(heads):
        cols = slice(h * HD, (h + 1) * HD)
        q0[h] = full[:, cols]
        q1[h] = l1[:, cols]
        q2[h] = l2[:, cols]
        q3[h] = l3[:, cols]
        q4[h] = l4[:, cols]
        q5[h] = l5[:, cols]
        q6[h] = l6[:, cols]

    to_right.wait_recv()
    relay_left = send(tokp.at[core, 0], tokp.at[core, 0], 8, twin)
    to_left.wait_recv()
    relay_right = send(tokp.at[core, 5], tokp.at[core, 5], 9, twin)
    relay_left.wait_recv()
    relay_right.wait_recv()

    for store, w in ((k0, wk_s), (v0, wv)):
        for b in (0, 5):
            full = dot(tokp[core, b], w[pl.ds(half, 512), :]) + dot(
                tokp[1 - core, b], w[pl.ds(other, 512), :]
            )
            full = full.astype(BF)
            for h in range(heads):
                store[h, b * B : (b + 1) * B] = full[:, h * HD : (h + 1) * HD]

    place = reversed_bits(lax.broadcasted_iota(jnp.int32, (1, B), 1))
    none = jnp.zeros((1, B), F32)
    biases = []
    for b in range(4):
        before = (me * 4 + b - 1) * B + place
        after = (me * 4 + b + 1) * B + place
        biases.append(
            jnp.concatenate(
                [
                    jnp.where(before >= start_ref[b], 0.0, -jnp.inf),
                    none,
                    jnp.where(after < end_ref[b], 0.0, -jnp.inf),
                ],
                axis=1,
            )
        )

    def near(h, carry):
        for b in range(4):
            c = b // 2
            o = (c ^ 1) * B
            rows = slice(b * B, (b + 1) * B)
            fine = attend(q0[h, rows], k0[h, b * B : (b + 3) * B], v0[h, b * B : (b + 3) * B], biases[b])
            coarse = attend(q1[h, b * 64 : (b + 1) * 64], k1[h, o : o + B], v1[h, o : o + B])
            state = merge(fine, tuple(twice(x, 1) for x in coarse))
            fpeak[h, rows], ftot[h, rows], fnum[h, rows] = state
        return carry

    lax.fori_loop(0, heads, near, 0)

    def landed(level):
        n = lands[level]
        pltpu.make_async_copy(n, n, recv_sem.at[level]).wait()

    for level in range(LEVELS, 1, -1):
        landed(level)

    def far(h, carry):
        k6 = r6[:, h].astype(F32).reshape(16, 2, 8, HD)
        six = attend(q6[h], k6[:, 0].reshape(B, HD).astype(BF), k6[:, 1].reshape(B, HD).astype(BF))
        state = merge(attend(q5[h], r5[:, h, 0].reshape(B, HD), r5[:, h, 1].reshape(B, HD)), six)
        state = merge(attend(q4[h], r4[:, h, 0].reshape(B, HD), r4[:, h, 1].reshape(B, HD)), state)
        state = tuple(twice(x, 4) for x in state)
        state = merge(attend(q3[h], r3[:, h, 0].reshape(B, HD), r3[:, h, 1].reshape(B, HD)), state)
        state = tuple(twice(x, 4) for x in state)
        state = merge(attend(q2[h], r2[h, 0], r2[h, 1]), state)
        cols = pl.ds(pl.multiple_of(h * HD, HD), HD)
        for b in range(4):
            rows = slice(b * B, (b + 1) * B)
            part = tuple(twice(twice(x[b * 32 : (b + 1) * 32], 1), 1) for x in state)
            peak, total, numer = merge((fpeak[h, rows], ftot[h, rows], fnum[h, rows]), part)
            out_ref[rows, cols] = dot(perm, (numer / total).astype(BF)).astype(BF)
        return carry

    lax.fori_loop(0, heads, far, 0)

    to_right.wait_send()
    to_left.wait_send()
    relay_left.wait_send()
    relay_right.wait_send()
    for level in range(2, LEVELS + 1):
        n = lands[level]
        pltpu.make_async_copy(n, n, send_sem.at[level]).wait()


def on_device(count, tokens, w_qk, w_value, span_start, span_end):
    rows, feats = tokens.shape
    heads = w_value.shape[1] // HD
    anywhere = pl.BlockSpec(memory_space=pl.ANY)
    scalar = pl.BlockSpec(memory_space=pltpu.SMEM)

    def vm(*shape, dtype=BF):
        return pltpu.VMEM(shape, dtype)

    width = heads * HD
    scratch = [
        vm(rows, feats), vm(2, 6, B, feats), vm(2 * feats, 2, width), vm(2 * feats, width),
        vm(2 * feats, width), vm(2 * feats, width), vm(3, rows, width, dtype=F32),
        vm(heads, rows, HD), vm(heads, rows + 2 * B, HD), vm(heads, rows + 2 * B, HD),
        vm(heads, 256, HD), vm(heads, 256, HD), vm(heads, 256, HD),
        vm(heads, 128, HD), vm(heads, 64, HD), vm(heads, 32, HD), vm(heads, 32, HD), vm(heads, 32, HD),
        vm(heads, 2, 128, HD), vm(heads, 2, 64, HD), vm(heads, 2, 32, HD), vm(heads, 2, 16, HD), vm(heads, 16, HD),
        vm(heads, 2, 128, HD), vm(2, heads, 2, 64, HD), vm(4, heads, 2, 32, HD), vm(8, heads, 2, 16, HD), vm(16, heads, 16, HD),
        vm(heads, rows, 1, dtype=F32), vm(heads, rows, 1, dtype=F32), vm(heads, rows, HD, dtype=F32),
        pltpu.SemaphoreType.DMA((3,)), pltpu.SemaphoreType.DMA((10,)), pltpu.SemaphoreType.DMA((10,)),
    ]
    return pl.pallas_call(
        functools.partial(kernel, count),
        out_shape=jax.ShapeDtypeStruct((rows, width), BF),
        in_specs=[anywhere, anywhere, anywhere, scalar, scalar],
        out_specs=pl.BlockSpec(memory_space=pltpu.VMEM),
        scratch_shapes=scratch,
        name="htransformer",
        cost_estimate=pl.CostEstimate(flops=3 * 10**9, bytes_accessed=5 * 10**6, transcendentals=10**6),
        compiler_params=pltpu.CompilerParams(
            collective_id=0, has_side_effects=True, vmem_limit_bytes=48 * 2**20
        ),
    )(tokens, w_qk, w_value, span_start, span_end)


def solution(mesh):
    placed = (P("seq", "head"), P(None, None, "head"), P(None, "head"), P("seq"), P("seq"))
    return jax.shard_map(
        functools.partial(on_device, mesh.shape["seq"]),
        mesh=mesh, in_specs=placed, out_specs=P("seq", "head"), check_vma=False,
    )
```

profile of v0, /device:TPU:1, one launch (start us, length us, event | category | flops | bytes accessed | tf_op | source)
XLA Modules:
  0.0 63.5 jit_solution(10709353036452042985)
XLA Ops:
  0.0 0.0 copy-start
  0.0 1.6 %copy-done = bf16[1024,2,512]{2,1,0:T(2,128)(2,1)S(1)} copy-done((bf16[1024,2,512]{2,1,0:T(2,128)(2,1)S(1)}, bf16[1024,2,512]{2,1,0:T(2,128)(2,1)}, u32[]{:S(2)}) %copy-start) | copy-done | bytes 2097176
  1.6 0.0 copy-start.1
  1.6 1.2 %copy-done.1 = bf16[1024,512]{1,0:T(8,128)(2,1)S(1)} copy-done((bf16[1024,512]{1,0:T(8,128)(2,1)S(1)}, bf16[1024,512]{1,0:T(8,128)(2,1)}, u32[]{:S(2)}) %copy-start.1) | copy-done | bytes 1048600
  2.8 0.0 copy-start.2
  2.8 1.0 %copy-done.2 = bf16[512,512]{1,0:T(8,128)(2,1)S(1)} copy-done((bf16[512,512]{1,0:T(8,128)(2,1)S(1)}, bf16[512,512]{1,0:T(8,128)(2,1)}, u32[]{:S(2)}) %copy-start.2) | copy-done | bytes 524312
  3.9 0.0 copy-start.3
  3.9 0.7 %copy-done.3 = s32[4]{0:T(128)S(1)} copy-done((s32[4]{0:T(128)S(1)}, s32[4]{0:T(128)}, u32[]{:S(2)}) %copy-start.3) | copy-done | bytes 40
  4.5 0.0 copy-start.4
  4.5 0.7 %copy-done.4 = s32[4]{0:T(128)S(1)} copy-done((s32[4]{0:T(128)S(1)}, s32[4]{0:T(128)}, u32[]{:S(2)}) %copy-start.4) | copy-done | bytes 40
  5.2 57.5 %htransformer.1 = bf16[512,512]{1,0:T(8,128)(2,1)S(1)} custom-call(bf16[512,512]{1,0:T(8,128)(2,1)S(1)} %copy-done.2, bf16[1024,2,512]{2,1,0:T(2,128)(2,1)S(1)} %copy-done, bf16[1024,512]{1,0:T(8,128)(2,1)S(1)} %copy-done.1, s32[4]{0:T(128)S(1)} %copy-done.3, s32[4]{0:T(128)S(1)} %copy-done.4), custom_call_target="tpu_custom_call" | custom-call | flops 3000000000 | bytes 5000000 | tf_op jit(solution)/shard_map/htransformer/pallas_call | solution.py:309
  62.7 0.8 %copy.7 = bf16[512,512]{1,0:T(8,128)(2,1)} copy(bf16[512,512]{1,0:T(8,128)(2,1)S(1)} %htransformer.1) | data formatting | bytes 1048576
Async XLA Ops:
  0.0 1.6 %copy-start = (bf16[1024,2,512]{2,1,0:T(2,128)(2,1)S(1)}, bf16[1024,2,512]{2,1,0:T(2,128)(2,1)}, u32[]{:S(2)}) copy-start(bf16[1024,2,512]{2,1,0:T(2,128)(2,1)} %wqk_hbm.1) | copy-start | bytes 6291460
  1.6 1.2 %copy-start.1 = (bf16[1024,512]{1,0:T(8,128)(2,1)S(1)}, bf16[1024,512]{1,0:T(8,128)(2,1)}, u32[]{:S(2)}) copy-start(bf16[1024,512]{1,0:T(8,128)(2,1)} %wv_hbm.1) | copy-start | bytes 3145732
  2.8 1.0 %copy-start.2 = (bf16[512,512]{1,0:T(8,128)(2,1)S(1)}, bf16[512,512]{1,0:T(8,128)(2,1)}, u32[]{:S(2)}) copy-start(bf16[512,512]{1,0:T(8,128)(2,1)} %tok_hbm.1) | copy-start | bytes 1572868
  3.9 0.7 %copy-start.3 = (s32[4]{0:T(128)S(1)}, s32[4]{0:T(128)}, u32[]{:S(2)}) copy-start(s32[4]{0:T(128)} %start_ref.1) | copy-start | bytes 52
  4.5 0.7 %copy-start.4 = (s32[4]{0:T(128)S(1)}, s32[4]{0:T(128)}, u32[]{:S(2)}) copy-start(s32[4]{0:T(128)} %end_ref.1) | copy-start | bytes 52
where the time goes:
time: 63.7 us; the launch traced here: 63.5 us
  Pallas kernels  57.5 us (90%)
  local copies, waits for them, and re-layouts  5.96 us (9%)
    pallas_call x1, Pallas kernels, on_device(): pl.pallas_call(functools.partial(kernel, count), out_shape=jax.ShapeDtype...  57.5 us
    unnamed x11, local copies, waits for them, and re-layouts  5.96 us

commit v1 on v0

--- a/solution.py
+++ b/solution.py
@@ -46,8 +46,9 @@
     if bias is not None:
         s = s + bias
     top = jnp.max(s, axis=-1, keepdims=True)
-    w = jnp.exp2((s - top) * UNIT)
-    return top * UNIT, jnp.sum(w, axis=-1, keepdims=True), dot(w.astype(BF), v)
+    w = jnp.exp2((s - top) * UNIT).astype(BF)
+    both = dot(w, jnp.concatenate([v, jnp.ones_like(v)], axis=1))
+    return jnp.broadcast_to(top * UNIT, (q.shape[0], HD)), both[:, HD:], both[:, :HD]
 
 
 def merge(a, b):
@@ -69,14 +70,14 @@
 
 def kernel(
     count,
-    tok_hbm, wqk_hbm, wv_hbm, start_ref, end_ref,
+    tok_hbm, wqk_hbm, wv_hbm, start_hbm, end_hbm,
     out_ref,
     tok_raw, tokp, wqk, wv, wq_s, wk_s, acc,
-    q0, k0, v0, q1, k1, v1, q2, q3, q4, q5, q6,
+    q0, k0, v0, q1, k1, v1, q2, q3, q4,
     s2, s3, s4, s5, s6,
-    r2, r3, r4, r5, r6,
+    r2, r3, r4, r5, r6, rq, sr, rr,
     fpeak, ftot, fnum,
-    load_sem, send_sem, recv_sem,
+    start_ref, end_ref, load_sem, send_sem, recv_sem,
 ):
     me, core = lax.axis_index("seq"), lax.axis_index("head")
     heads = q0.shape[0]
@@ -87,6 +88,8 @@
         pltpu.make_async_copy(tok_hbm, tok_raw, load_sem.at[0]),
         pltpu.make_async_copy(wqk_hbm, wqk, load_sem.at[1]),
         pltpu.make_async_copy(wv_hbm, wv, load_sem.at[2]),
+        pltpu.make_async_copy(start_hbm, start_ref, load_sem.at[3]),
+        pltpu.make_async_copy(end_hbm, end_ref, load_sem.at[4]),
     ]
     for load in loads:
         load.start()
@@ -123,8 +126,15 @@
     to_left = send(tokp.at[core, 1], tokp.at[core, 5], 7, (left, core))
 
     loads[1].wait()
-    wq_s[...] = wqk[:, 0, :]
-    wk_s[...] = wqk[:, 1, :]
+
+    def split(i, carry):
+        rows = pl.ds(pl.multiple_of(i * 64, 64), 64)
+        pair = jnp.swapaxes(wqk[rows], 0, 1)
+        wq_s[rows, :] = pair[0]
+        wk_s[rows, :] = pair[1]
+        return carry
+
+    lax.fori_loop(0, wqk.shape[0] // 64, split, 0)
     loads[2].wait()
 
     half = pl.multiple_of(core * 512, 512)
@@ -137,12 +147,8 @@
     swap.wait()
     theirs = tokp[1 - core, 1:5].reshape(4 * B, 512)
 
-    quarter_row = lax.broadcasted_iota(jnp.int32, (32, 32), 0)
-    quarter_col = lax.broadcasted_iota(jnp.int32, (32, 32), 1)
-
-    def mix(rows, apart):
-        r, c = quarter_row[:rows], quarter_col[:rows]
-        return jnp.where((c == r) | (c == (r ^ apart)), 0.5, 0.0).astype(BF)
+    def mix(apart):
+        return jnp.where((col == row) | (col == (row ^ apart)), 0.5, 0.0).astype(BF)
 
     def narrow():
         r = lax.broadcasted_iota(jnp.int32, (16, 32), 0)
@@ -182,18 +188,18 @@
     for h in range(heads):
         s6[h] = both[:, h * HD : (h + 1) * HD]
 
+    for level in range(LEVELS, 3, -1):
+        for p in siblings(me, level):
+            send(sends[level].at[p % 4], lands[level].at[me % group(level)], level, (p, core))
+    for p in siblings(me, 3):
+        send(s3, r3.at[me % 2], 3, (p, core))
     send(s2, r2, 2, (siblings(me, 2)[0], core))
-    for level in range(3, LEVELS + 1):
-        for p in siblings(me, level):
-            send(sends[level], lands[level].at[me % group(level)], level, (p, core))
 
     full = (acc[2] + dot(theirs, wq_s[pl.ds(other, 512), :])).astype(BF)
     l1 = pool_halves(full.astype(F32), 4)
     l2 = pool_halves(l1.astype(F32), 4)
     l3 = pool_halves(l2.astype(F32), 4)
     l4 = pool_halves(l3.astype(F32), 4)
-    l5 = dot(mix(32, 4), l4).astype(BF)
-    l6 = dot(mix(32, 2), l5).astype(BF)
     for h in range(heads):
         cols = slice(h * HD, (h + 1) * HD)
         q0[h] = full[:, cols]
@@ -201,8 +207,11 @@
         q2[h] = l2[:, cols]
         q3[h] = l3[:, cols]
         q4[h] = l4[:, cols]
-        q5[h] = l5[:, cols]
-        q6[h] = l6[:, cols]
+    mine4 = me % 4
+    mates = [me - mine4 + (mine4 + k) % 4 for k in range(1, 4)]
+    for p in mates:
+        send(q4.at[p % 4], rq.at[mine4], 10, (p, core))
+    rq[mine4] = q4[mine4]
 
     to_right.wait_recv()
     relay_left = send(tokp.at[core, 0], tokp.at[core, 0], 8, twin)
@@ -220,8 +229,34 @@
             for h in range(heads):
                 store[h, b * B : (b + 1) * B] = full[:, h * HD : (h + 1) * HD]
 
+    def landed(level):
+        n = lands[level]
+        pltpu.make_async_copy(n, n, recv_sem.at[level]).wait()
+
+    landed(6)
+    landed(5)
+    landed(4)
+    pltpu.make_async_copy(rq.at[pl.ds(0, 3)], rq.at[pl.ds(0, 3)], recv_sem.at[10]).wait()
+    four = rq[...].reshape(B, HD)
+    five = dot(mix(4), four).astype(BF)
+    six = dot(mix(2), five).astype(BF)
+    pairs = r6[...].astype(F32).reshape(16, 2, 8, HD)
+    state = attend(six, pairs[:, 0].reshape(B, HD).astype(BF), pairs[:, 1].reshape(B, HD).astype(BF))
+    state = merge(attend(five, r5[:, 0].reshape(B, HD), r5[:, 1].reshape(B, HD)), state)
+    state = merge(attend(four, r4[:, 0].reshape(B, HD), r4[:, 1].reshape(B, HD)), state)
+    line = [jnp.sum(jnp.where(row == col, x, 0.0), axis=0, keepdims=True) for x in state[:2]]
+    stats = jnp.where(row[:8] == 0, line[0], line[1])
+    for j in range(4):
+        sr[j, :32] = state[2][j * 32 : (j + 1) * 32]
+        sr[j, 32:] = stats
+    for p in mates:
+        send(sr.at[p % 4], rr.at[mine4], 11, (p, core))
+    rr[mine4] = sr[mine4]
+
     place = reversed_bits(lax.broadcasted_iota(jnp.int32, (1, B), 1))
     none = jnp.zeros((1, B), F32)
+    loads[3].wait()
+    loads[4].wait()
     biases = []
     for b in range(4):
         before = (me * 4 + b - 1) * B + place
@@ -250,18 +285,17 @@
 
     lax.fori_loop(0, heads, near, 0)
 
-    def landed(level):
-        n = lands[level]
-        pltpu.make_async_copy(n, n, recv_sem.at[level]).wait()
-
-    for level in range(LEVELS, 1, -1):
-        landed(level)
+    landed(3)
+    pltpu.make_async_copy(rr.at[pl.ds(0, 3)], rr.at[pl.ds(0, 3)], recv_sem.at[11]).wait()
+    landed(2)
 
     def far(h, carry):
-        k6 = r6[:, h].astype(F32).reshape(16, 2, 8, HD)
-        six = attend(q6[h], k6[:, 0].reshape(B, HD).astype(BF), k6[:, 1].reshape(B, HD).astype(BF))
-        state = merge(attend(q5[h], r5[:, h, 0].reshape(B, HD), r5[:, h, 1].reshape(B, HD)), six)
-        state = merge(attend(q4[h], r4[:, h, 0].reshape(B, HD), r4[:, h, 1].reshape(B, HD)), state)
+        own = col[:32] == mine4 * 32 + row[:32]
+        stats = [
+            jnp.sum(jnp.where(own, rr[h, 32 + i : 33 + i], 0.0), axis=1, keepdims=True)
+            for i in range(2)
+        ]
+        state = tuple(jnp.broadcast_to(x, (32, HD)) for x in stats) + (rr[h, :32],)
         state = tuple(twice(x, 4) for x in state)
         state = merge(attend(q3[h], r3[:, h, 0].reshape(B, HD), r3[:, h, 1].reshape(B, HD)), state)
         state = tuple(twice(x, 4) for x in state)
@@ -283,13 +317,14 @@
     for level in range(2, LEVELS + 1):
         n = lands[level]
         pltpu.make_async_copy(n, n, send_sem.at[level]).wait()
+    pltpu.make_async_copy(rq.at[pl.ds(0, 3)], rq.at[pl.ds(0, 3)], send_sem.at[10]).wait()
+    pltpu.make_async_copy(sr.at[pl.ds(0, 3)], sr.at[pl.ds(0, 3)], send_sem.at[11]).wait()
 
 
 def on_device(count, tokens, w_qk, w_value, span_start, span_end):
     rows, feats = tokens.shape
     heads = w_value.shape[1] // HD
-    anywhere = pl.BlockSpec(memory_space=pl.ANY)
-    scalar = pl.BlockSpec(memory_space=pltpu.SMEM)
+    anywhere = pl.BlockSpec(memory_space=pltpu.HBM)
 
     def vm(*shape, dtype=BF):
         return pltpu.VMEM(shape, dtype)
@@ -300,22 +335,24 @@
         vm(2 * feats, width), vm(2 * feats, width), vm(3, rows, width, dtype=F32),
         vm(heads, rows, HD), vm(heads, rows + 2 * B, HD), vm(heads, rows + 2 * B, HD),
         vm(heads, 256, HD), vm(heads, 256, HD), vm(heads, 256, HD),
-        vm(heads, 128, HD), vm(heads, 64, HD), vm(heads, 32, HD), vm(heads, 32, HD), vm(heads, 32, HD),
+        vm(heads, 128, HD), vm(heads, 64, HD), vm(heads, 32, HD),
         vm(heads, 2, 128, HD), vm(heads, 2, 64, HD), vm(heads, 2, 32, HD), vm(heads, 2, 16, HD), vm(heads, 16, HD),
-        vm(heads, 2, 128, HD), vm(2, heads, 2, 64, HD), vm(4, heads, 2, 32, HD), vm(8, heads, 2, 16, HD), vm(16, heads, 16, HD),
-        vm(heads, rows, 1, dtype=F32), vm(heads, rows, 1, dtype=F32), vm(heads, rows, HD, dtype=F32),
-        pltpu.SemaphoreType.DMA((3,)), pltpu.SemaphoreType.DMA((10,)), pltpu.SemaphoreType.DMA((10,)),
+        vm(heads, 2, 128, HD), vm(2, heads, 2, 64, HD), vm(4, 2, 32, HD), vm(8, 2, 16, HD), vm(16, 16, HD),
+        vm(4, 32, HD), vm(4, 40, HD, dtype=F32), vm(heads, 40, HD, dtype=F32),
+        vm(heads, rows, HD, dtype=F32), vm(heads, rows, HD, dtype=F32), vm(heads, rows, HD, dtype=F32),
+        pltpu.SMEM((4,), jnp.int32), pltpu.SMEM((4,), jnp.int32),
+        pltpu.SemaphoreType.DMA((5,)), pltpu.SemaphoreType.DMA((12,)), pltpu.SemaphoreType.DMA((12,)),
     ]
     return pl.pallas_call(
         functools.partial(kernel, count),
         out_shape=jax.ShapeDtypeStruct((rows, width), BF),
-        in_specs=[anywhere, anywhere, anywhere, scalar, scalar],
+        in_specs=[anywhere] * 5,
         out_specs=pl.BlockSpec(memory_space=pltpu.VMEM),
         scratch_shapes=scratch,
         name="htransformer",
         cost_estimate=pl.CostEstimate(flops=3 * 10**9, bytes_accessed=5 * 10**6, transcendentals=10**6),
         compiler_params=pltpu.CompilerParams(
-            collective_id=0, has_side_effects=True, vmem_limit_bytes=48 * 2**20
+            collective_id=0, has_side_effects=True, vmem_limit_bytes=56 * 2**20
         ),
     )(tokens, w_qk, w_value, span_start, span_end)
 

time: 63.7 us -> 45.4 us (0.71)
  Pallas kernels: 57.5 us -> 43.4 us
  local copies, waits for them, and re-layouts: 5.96 us -> 1.87 us
    pallas_call x1, Pallas kernels: 57.5 us -> 43.4 us  [on_device(): pl.pallas_call(functools.partial(kernel, count), out_shape=jax.ShapeDtype...]
    unnamed x11 -> x1, local copies, waits for them, and re-layouts: 5.96 us -> 1.87 us
where the time goes in v1:
time: 45.4 us; the launch traced here: 45.3 us
  Pallas kernels  43.4 us (96%)
  local copies, waits for them, and re-layouts  1.87 us (4%)
    pallas_call x1, Pallas kernels, on_device(): pl.pallas_call(functools.partial(kernel, count), out_shape=jax.ShapeDtype...  43.4 us
    unnamed x1, local copies, waits for them, and re-layouts  1.87 us

profile of v1, /device:TPU:1, one launch (start us, length us, event | category | flops | bytes accessed | tf_op | source)
XLA Modules:
  0.0 45.3 jit_solution(6191234226569381562)
XLA Ops:
  0.0 43.4 %htransformer.1 = bf16[512,512]{1,0:T(8,128)(2,1)} custom-call(bf16[512,512]{1,0:T(8,128)(2,1)} %tok_hbm.1, bf16[1024,2,512]{2,1,0:T(2,128)(2,1)} %wqk_hbm.1, bf16[1024,512]{1,0:T(8,128)(2,1)} %wv_hbm.1, s32[4]{0:T(128)} %start_hbm.1, s32[4]{0:T(128)} %end_hbm.1), custom_call_target="tpu_custom_call" | custom-call | flops 3000000000 | bytes 5000000 | tf_op jit(solution)/shard_map/htransformer/pallas_call | solution.py:346
  43.4 1.9 %copy.7 = bf16[512,512]{1,0:T(8,128)(2,1)} copy(bf16[512,512]{1,0:T(8,128)(2,1)} %htransformer.1) | data formatting | bytes 1048576

commit v2 on v0

v2 whole, which is shorter than its diff:
```python
import functools
import math

import jax
import jax.numpy as jnp
from jax import lax
from jax.experimental import pallas as pl
from jax.experimental.pallas import tpu as pltpu
from jax.sharding import PartitionSpec as P

HD = 128
B = 128
NEAR_FIRST = 2
MESH = pl.DeviceIdType.MESH
BF = jnp.bfloat16
F32 = jnp.float32
UNIT = math.log2(math.e) / math.sqrt(HD)


def reversed_bits(x, bits=7):
    out = jnp.zeros_like(x)
    for i in range(bits):
        out = out + (((x >> i) & 1) << (bits - 1 - i))
    return out


def dot(a, b):
    return jnp.dot(a, b, preferred_element_type=F32)


def pool_halves(x, blocks):
    rows, cols = x.shape
    y = x.reshape(blocks, 2, rows // (2 * blocks), cols)
    y = (y[:, 0] + y[:, 1]) * 0.5
    return y.reshape(rows // 2, cols).astype(BF)


def twice(x, blocks):
    rows, cols = x.shape
    y = x.reshape(blocks, rows // blocks, cols)
    return jnp.concatenate([y, y], axis=1).reshape(2 * rows, cols)


def attend(q, k, v, bias=None):
    s = lax.dot_general(q, k, (((1,), (1,)), ((), ())), preferred_element_type=F32)
    if bias is not None:
        s = s + bias
    top = jnp.max(s, axis=-1, keepdims=True)
    w = jnp.exp2((s - top) * UNIT).astype(BF)
    both = dot(w, jnp.concatenate([v, jnp.ones_like(v)], axis=1))
    return jnp.broadcast_to(top * UNIT, (q.shape[0], HD)), both[:, HD:], both[:, :HD]


def merge(a, b):
    top = jnp.maximum(a[0], b[0])
    ka, kb = jnp.exp2(a[0] - top), jnp.exp2(b[0] - top)
    return top, a[1] * ka + b[1] * kb, a[2] * ka + b[2] * kb


def pool_matrix(rows, run):
    r = lax.broadcasted_iota(jnp.int32, (rows, 2 * rows), 0)
    c = lax.broadcasted_iota(jnp.int32, (rows, 2 * rows), 1)
    first = (r // run) * (2 * run) + r % run
    return jnp.where((c == first) | (c == first + run), 0.5, 0.0).astype(BF)


def kernel(
    count,
    tok_hbm, wqk_hbm, wv_hbm, span_hbm,
    out_ref,
    tok_raw, tokp, wqk, wv, wq_s, wk_s, acc,
    q0, k0, v0, q1, k1, v1, q2,
    s2, s3, s4, s5, s6, sr,
    r2, r3, r4, r5, r6, rr,
    fpeak, ftot, fnum,
    span, load_sem, send_sem, recv_sem,
):
    me, core = lax.axis_index("seq"), lax.axis_index("head")
    heads = q0.shape[0]

    loads = [
        pltpu.make_async_copy(tok_hbm, tok_raw, load_sem.at[0]),
        pltpu.make_async_copy(wqk_hbm, wqk, load_sem.at[1]),
        pltpu.make_async_copy(wv_hbm, wv, load_sem.at[2]),
        pltpu.make_async_copy(span_hbm, span, load_sem.at[3]),
    ]
    for load in loads:
        load.start()

    def flip(device, bit):
        return device + bit * (1 - 2 * ((device // bit) % 2))

    def mirror(device):
        return device + 7 - 2 * (device % 8)

    def head_of(device):
        place = device % 4
        return place + ((device // 4) % 2) * (3 - 2 * place)

    right, left = (me + 1) % count, (me + count - 1) % count
    twin = (me, 1 - core)
    place4 = me % 4
    mates = [me - place4 + (place4 + k) % 4 for k in (1, 2, 3)]
    over5 = [flip(me, 8), mirror(flip(me, 8))]
    across = flip(me, 16)
    over6 = [across, flip(across, 8), mirror(across), mirror(flip(across, 8))]
    greet = [twin] + [(p, core) for p in [right, left, mirror(me)] + mates + over5 + over6]
    barrier = pltpu.get_barrier_semaphore()
    for device in greet:
        pl.semaphore_signal(barrier, inc=1, device_id=device, device_id_type=MESH)

    row = lax.broadcasted_iota(jnp.int32, (B, B), 0)
    col = lax.broadcasted_iota(jnp.int32, (B, B), 1)
    perm = jnp.where(reversed_bits(row) == col, 1.0, 0.0).astype(BF)

    loads[0].wait()
    for b in range(4):
        tokp[core, b + 1] = dot(perm, tok_raw[b * B : (b + 1) * B]).astype(BF)

    pl.semaphore_wait(barrier, len(greet))

    def send(src, dst, sem, device):
        copy = pltpu.make_async_remote_copy(
            src_ref=src, dst_ref=dst, send_sem=send_sem.at[sem], recv_sem=recv_sem.at[sem],
            device_id=device, device_id_type=MESH,
        )
        copy.start()
        return copy

    def arrived(ref, sem):
        pltpu.make_async_copy(ref, ref, recv_sem.at[sem]).wait()

    def gone(ref, sem):
        pltpu.make_async_copy(ref, ref, send_sem.at[sem]).wait()

    swap = send(tokp.at[core, pl.ds(1, 4)], tokp.at[core, pl.ds(1, 4)], 0, twin)
    to_right = send(tokp.at[core, 4], tokp.at[core, 0], 1, (right, core))
    to_left = send(tokp.at[core, 1], tokp.at[core, 5], 7, (left, core))

    loads[1].wait()

    def split(i, carry):
        rows = pl.ds(pl.multiple_of(i * 64, 64), 64)
        pair = jnp.swapaxes(wqk[rows], 0, 1)
        wq_s[rows, :] = pair[0]
        wk_s[rows, :] = pair[1]
        return carry

    lax.fori_loop(0, wqk.shape[0] // 64, split, 0)
    loads[2].wait()

    half = pl.multiple_of(core * 512, 512)
    other = pl.multiple_of((1 - core) * 512, 512)
    weights = (wk_s, wv, wq_s)
    mine = tokp[core, 1:5].reshape(4 * B, 512)
    for i, w in enumerate(weights):
        acc[i] = dot(mine, w[pl.ds(half, 512), :])

    swap.wait()
    theirs = tokp[1 - core, 1:5].reshape(4 * B, 512)

    for i in range(3):
        full = (acc[i] + dot(theirs, weights[i][pl.ds(other, 512), :])).astype(BF)
        l1 = pool_halves(full.astype(F32), 4)
        l2 = pool_halves(l1.astype(F32), 4)
        l3 = pool_halves(l2.astype(F32), 4)
        for h in range(heads):
            cols = slice(h * HD, (h + 1) * HD)
            s3[h, i] = l3[:, cols]
            if i < 2:
                (k0, v0)[i][h, B : 5 * B] = full[:, cols]
                (k1, v1)[i][h] = l1[:, cols]
                s2[h, i] = l2[:, cols]
            else:
                q0[h] = full[:, cols]
                q1[h] = l1[:, cols]
                q2[h] = l2[:, cols]

    my_head = head_of(me)
    for p in mates:
        send(s3.at[head_of(p)], r3.at[place4], 3, (p, core))
    send(s2, r2, 2, (flip(me, 1), core))
    r3[place4] = s3[my_head]

    to_right.wait_recv()
    relay_left = send(tokp.at[core, 0], tokp.at[core, 0], 8, twin)
    to_left.wait_recv()
    relay_right = send(tokp.at[core, 5], tokp.at[core, 5], 9, twin)
    relay_left.wait_recv()
    relay_right.wait_recv()

    for store, w in ((k0, wk_s), (v0, wv)):
        for b in (0, 5):
            full = dot(tokp[core, b], w[pl.ds(half, 512), :]) + dot(
                tokp[1 - core, b], w[pl.ds(other, 512), :]
            )
            full = full.astype(BF)
            for h in range(heads):
                store[h, b * B : (b + 1) * B] = full[:, h * HD : (h + 1) * HD]

    turned = reversed_bits(lax.broadcasted_iota(jnp.int32, (1, B), 1))
    none = jnp.zeros((1, B), F32)
    loads[3].wait()
    biases = []
    for b in range(4):
        before = (me * 4 + b - 1) * B + turned
        after = (me * 4 + b + 1) * B + turned
        biases.append(
            jnp.concatenate(
                [
                    jnp.where(before >= span[0, b], 0.0, -jnp.inf),
                    none,
                    jnp.where(after < span[1, b], 0.0, -jnp.inf),
                ],
                axis=1,
            )
        )

    def near(h, carry):
        for b in range(4):
            c = b // 2
            o = (c ^ 1) * B
            rows = slice(b * B, (b + 1) * B)
            fine = attend(q0[h, rows], k0[h, b * B : (b + 3) * B], v0[h, b * B : (b + 3) * B], biases[b])
            coarse = attend(q1[h, b * 64 : (b + 1) * 64], k1[h, o : o + B], v1[h, o : o + B])
            state = merge(fine, tuple(twice(x, 1) for x in coarse))
            fpeak[h, rows], ftot[h, rows], fnum[h, rows] = state
        return carry

    lax.fori_loop(0, NEAR_FIRST, near, 0)

    arrived(r3.at[pl.ds(0, 3)], 3)
    five_rows, six_rows = pool_matrix(64, 4), pool_matrix(32, 2)
    for i in range(2):
        l4 = pool_halves(r3[:, i].astype(F32).reshape(2 * B, HD), 16)
        l5 = dot(five_rows, l4).astype(BF)
        s4[i] = l4
        s5[i] = l5
        s6[i] = dot(six_rows, l5).astype(BF)
    for p in over6:
        send(s6, r6.at[(me // 4) % 4], 6, (p, core))
    for p in over5:
        send(s5, r5.at[(me // 4) % 2], 5, (p, core))
    send(s4, r4, 4, (mirror(me), core))

    queries = r3[:, 2]
    three = [
        attend(
            queries[2 * c : 2 * c + 2].reshape(B, HD),
            r3[2 - 2 * c : 4 - 2 * c, 0].reshape(B, HD),
            r3[2 - 2 * c : 4 - 2 * c, 1].reshape(B, HD),
        )
        for c in range(2)
    ]
    four = pool_halves(queries.astype(F32).reshape(2 * B, HD), 16)

    def mix(apart):
        return jnp.where((col == row) | (col == (row ^ apart)), 0.5, 0.0).astype(BF)

    five = dot(mix(4), four).astype(BF)
    six = dot(mix(2), five).astype(BF)

    lax.fori_loop(NEAR_FIRST, heads, near, 0)

    arrived(r2, 2)

    def second(h, carry):
        state = attend(q2[h], r2[h, 0], r2[h, 1])
        for b in range(4):
            rows = slice(b * B, (b + 1) * B)
            part = tuple(twice(twice(x[b * 32 : (b + 1) * 32], 1), 1) for x in state)
            peak, total, numer = merge((fpeak[h, rows], ftot[h, rows], fnum[h, rows]), part)
            fnum[h, rows] = numer / total
            fpeak[h, rows] = peak + jnp.log2(total)
        return carry

    lax.fori_loop(0, heads, second, 0)

    arrived(r6, 6)
    state = attend(six, r6[:, 0].reshape(B, HD), r6[:, 1].reshape(B, HD))
    arrived(r5, 5)
    state = merge(attend(five, r5[:, 0].reshape(B, HD), r5[:, 1].reshape(B, HD)), state)
    arrived(r4, 4)
    state = merge(attend(four, r4[0], r4[1]), state)
    lines = []
    for c in range(2):
        part = tuple(twice(x[c * 64 : (c + 1) * 64], 8) for x in state)
        peak, total, numer = merge(three[c], part)
        result = numer / total
        level = peak + jnp.log2(total)
        lines.append(jnp.sum(jnp.where(row == col, level, 0.0), axis=0, keepdims=True))
        sr[2 * c, :64] = result[:64]
        sr[2 * c + 1, :64] = result[64:]
    stats = jnp.where(row[:8] == 0, lines[0], lines[1])
    for j in range(4):
        sr[j, 64:] = stats
    for p in mates:
        send(sr.at[p % 4], rr.at[my_head], 10, (p, core))
    rr[my_head] = sr[place4]
    arrived(rr.at[pl.ds(0, 3)], 10)

    own = col[:64] == (place4 % 2) * 64 + row[:64]

    def last(h, carry):
        line = rr[h, pl.ds(64 + place4 // 2, 1)]
        level = jnp.sum(jnp.where(own, line, 0.0), axis=1, keepdims=True)
        level = jnp.broadcast_to(level, (64, HD))
        cols = pl.ds(pl.multiple_of(h * HD, HD), HD)
        for b in range(4):
            rows = slice(b * B, (b + 1) * B)
            far, far_level = rr[h, b * 16 : (b + 1) * 16], level[b * 16 : (b + 1) * 16]
            for _ in range(3):
                far, far_level = twice(far, 1), twice(far_level, 1)
            close = fnum[h, rows]
            share = 1.0 / (1.0 + jnp.exp2(fpeak[h, rows] - far_level))
            mixed = close + (far - close) * share
            out_ref[rows, cols] = dot(perm, mixed.astype(BF)).astype(BF)
        return carry

    lax.fori_loop(0, heads, last, 0)

    to_right.wait_send()
    to_left.wait_send()
    relay_left.wait_send()
    relay_right.wait_send()
    gone(r2, 2)
    gone(r3.at[pl.ds(0, 3)], 3)
    gone(r4, 4)
    gone(r5, 5)
    gone(r6, 6)
    gone(rr.at[pl.ds(0, 3)], 10)


def on_device(count, tokens, w_qk, w_value, span_start, span_end):
    rows, feats = tokens.shape
    heads = w_value.shape[1] // HD
    anywhere = pl.BlockSpec(memory_space=pltpu.HBM)

    def vm(*shape, dtype=BF):
        return pltpu.VMEM(shape, dtype)

    width = heads * HD
    scratch = [
        vm(rows, feats), vm(2, 6, B, feats), vm(2 * feats, 2, width), vm(2 * feats, width),
        vm(2 * feats, width), vm(2 * feats, width), vm(3, rows, width, dtype=F32),
        vm(heads, rows, HD), vm(heads, rows + 2 * B, HD), vm(heads, rows + 2 * B, HD),
        vm(heads, 256, HD), vm(heads, 256, HD), vm(heads, 256, HD), vm(heads, 128, HD),
        vm(heads, 2, 128, HD), vm(heads, 3, 64, HD), vm(2, 128, HD), vm(2, 64, HD), vm(2, 32, HD),
        vm(4, 72, HD, dtype=F32),
        vm(heads, 2, 128, HD), vm(4, 3, 64, HD), vm(2, 128, HD), vm(2, 2, 64, HD), vm(4, 2, 32, HD),
        vm(heads, 72, HD, dtype=F32),
        vm(heads, rows, HD, dtype=F32), vm(heads, rows, HD, dtype=F32), vm(heads, rows, HD, dtype=F32),
        pltpu.SMEM((2, 4), jnp.int32),
        pltpu.SemaphoreType.DMA((4,)), pltpu.SemaphoreType.DMA((11,)), pltpu.SemaphoreType.DMA((11,)),
    ]
    return pl.pallas_call(
        functools.partial(kernel, count),
        out_shape=jax.ShapeDtypeStruct((rows, width), BF),
        in_specs=[anywhere] * 4,
        out_specs=pl.BlockSpec(memory_space=pltpu.VMEM),
        scratch_shapes=scratch,
        name="htransformer",
        cost_estimate=pl.CostEstimate(flops=3 * 10**9, bytes_accessed=5 * 10**6, transcendentals=10**6),
        compiler_params=pltpu.CompilerParams(
            collective_id=0, has_side_effects=True, vmem_limit_bytes=53 * 2**20
        ),
    )(tokens, w_qk, w_value, jnp.stack([span_start, span_end]))


def solution(mesh):
    placed = (P("seq", "head"), P(None, None, "head"), P(None, "head"), P("seq"), P("seq"))
    return jax.shard_map(
        functools.partial(on_device, mesh.shape["seq"]),
        mesh=mesh, in_specs=placed, out_specs=P("seq", "head"), check_vma=False,
    )
```

time: 63.7 us -> 35.8 us (0.56)
  Pallas kernels: 57.5 us -> 34.2 us
  local copies, waits for them, and re-layouts: 5.96 us -> 0.8 us
  other arithmetic: 0 us -> 0.68 us
    pallas_call x1, Pallas kernels: 57.5 us -> 34.2 us  [on_device(): pl.pallas_call(functools.partial(kernel, count), out_shape=jax.ShapeDtype...]
    unnamed x11 -> x1, local copies, waits for them, and re-layouts: 5.96 us -> 0.8 us
    another operation x0 -> x1, other arithmetic: none -> 0.68 us  [on_device(): jnp.stack([span_start, span_end])]
where the time goes in v2:
time: 35.8 us; the launch traced here: 35.7 us
  Pallas kernels  34.2 us (96%)
  local copies, waits for them, and re-layouts  0.8 us (2%)
  other arithmetic  0.68 us (2%)
    pallas_call x1, Pallas kernels, on_device(): pl.pallas_call(functools.partial(kernel, count), out_shape=jax.ShapeDtype...  34.2 us
    unnamed x1, local copies, waits for them, and re-layouts  0.8 us

profile of v2, /device:TPU:1, one launch (start us, length us, event | category | flops | bytes accessed | tf_op | source)
XLA Modules:
  0.0 35.7 jit_solution(1780513171849046529)
XLA Ops:
  0.0 0.7 %pad_add_fusion.span_hbm = s32[2,4]{1,0:T(2,128)S(1)} fusion(s32[1,4]{1,0:T(1,128)} %bitcast.2, s32[1,4]{1,0:T(1,128)} %bitcast.3), kind=kLoop, calls=%fused_computation | loop fusion | flops 8 | bytes 64 | tf_op jit(solution)/shard_map/stack | solution.py:367
  0.7 34.2 %htransformer.1 = bf16[512,512]{1,0:T(8,128)(2,1)S(1)} custom-call(bf16[512,512]{1,0:T(8,128)(2,1)} %tok_hbm.1, bf16[1024,2,512]{2,1,0:T(2,128)(2,1)} %wqk_hbm.1, bf16[1024,512]{1,0:T(8,128)(2,1)} %wv_hbm.1, s32[2,4]{1,0:T(2,128)S(1)} %pad_add_fusion.span_hbm), custom_call_target="tpu_custom_call" | custom-call | flops 3000000000 | bytes 5000000 | tf_op jit(solution)/shard_map/htransformer/pallas_call | solution.py:356
  34.9 0.8 %copy.7 = bf16[512,512]{1,0:T(8,128)(2,1)} copy(bf16[512,512]{1,0:T(8,128)(2,1)S(1)} %htransformer.1) | data formatting | bytes 1048576

commit v3 on v2

--- a/solution.py
+++ b/solution.py
@@ -68,7 +68,7 @@
     count,
     tok_hbm, wqk_hbm, wv_hbm, span_hbm,
     out_ref,
-    tok_raw, tokp, wqk, wv, wq_s, wk_s, acc,
+    raw, tokp, wqk, wv, wq_s, wk_s, acc,
     q0, k0, v0, q1, k1, v1, q2,
     s2, s3, s4, s5, s6, sr,
     r2, r3, r4, r5, r6, rr,
@@ -76,10 +76,10 @@
     span, load_sem, send_sem, recv_sem,
 ):
     me, core = lax.axis_index("seq"), lax.axis_index("head")
-    heads = q0.shape[0]
+    heads, rows = q0.shape[0], q0.shape[1]
 
     loads = [
-        pltpu.make_async_copy(tok_hbm, tok_raw, load_sem.at[0]),
+        pltpu.make_async_copy(tok_hbm, raw.at[core, pl.ds(B, rows)], load_sem.at[0]),
         pltpu.make_async_copy(wqk_hbm, wqk, load_sem.at[1]),
         pltpu.make_async_copy(wv_hbm, wv, load_sem.at[2]),
         pltpu.make_async_copy(span_hbm, span, load_sem.at[3]),
@@ -113,10 +113,6 @@
     col = lax.broadcasted_iota(jnp.int32, (B, B), 1)
     perm = jnp.where(reversed_bits(row) == col, 1.0, 0.0).astype(BF)
 
-    loads[0].wait()
-    for b in range(4):
-        tokp[core, b + 1] = dot(perm, tok_raw[b * B : (b + 1) * B]).astype(BF)
-
     pl.semaphore_wait(barrier, len(greet))
 
     def send(src, dst, sem, device):
@@ -133,10 +129,16 @@
     def gone(ref, sem):
         pltpu.make_async_copy(ref, ref, send_sem.at[sem]).wait()
 
-    swap = send(tokp.at[core, pl.ds(1, 4)], tokp.at[core, pl.ds(1, 4)], 0, twin)
-    to_right = send(tokp.at[core, 4], tokp.at[core, 0], 1, (right, core))
-    to_left = send(tokp.at[core, 1], tokp.at[core, 5], 7, (left, core))
-
+    swap = send(tok_hbm, raw.at[core, pl.ds(B, rows)], 0, twin)
+    to_right = send(tok_hbm.at[pl.ds(rows - B, B)], raw.at[core, pl.ds(0, B)], 1, (right, core))
+    to_left = send(tok_hbm.at[pl.ds(0, B)], raw.at[core, pl.ds(rows + B, B)], 7, (left, core))
+
+    def turn(side, b):
+        tokp[side, b] = dot(perm, raw[side, b * B : (b + 1) * B]).astype(BF)
+
+    loads[0].wait()
+    for b in range(1, 5):
+        turn(core, b)
     loads[1].wait()
 
     def split(i, carry):
@@ -157,6 +159,8 @@
         acc[i] = dot(mine, w[pl.ds(half, 512), :])
 
     swap.wait()
+    for b in range(1, 5):
+        turn(1 - core, b)
     theirs = tokp[1 - core, 1:5].reshape(4 * B, 512)
 
     for i in range(3):
@@ -183,11 +187,45 @@
     r3[place4] = s3[my_head]
 
     to_right.wait_recv()
-    relay_left = send(tokp.at[core, 0], tokp.at[core, 0], 8, twin)
+    relay_left = send(raw.at[core, pl.ds(0, B)], raw.at[core, pl.ds(0, B)], 8, twin)
     to_left.wait_recv()
-    relay_right = send(tokp.at[core, 5], tokp.at[core, 5], 9, twin)
+    relay_right = send(raw.at[core, pl.ds(rows + B, B)], raw.at[core, pl.ds(rows + B, B)], 9, twin)
+    arrived(r3.at[pl.ds(0, 3)], 3)
+    five_rows, six_rows = pool_matrix(64, 4), pool_matrix(32, 2)
+    for i in range(2):
+        l4 = pool_halves(r3[:, i].astype(F32).reshape(2 * B, HD), 16)
+        l5 = dot(five_rows, l4).astype(BF)
+        s4[i] = l4
+        s5[i] = l5
+        s6[i] = dot(six_rows, l5).astype(BF)
+    for p in over6:
+        send(s6, r6.at[(me // 4) % 4], 6, (p, core))
+    for p in over5:
+        send(s5, r5.at[(me // 4) % 2], 5, (p, core))
+    send(s4, r4, 4, (mirror(me), core))
+
+    queries = r3[:, 2]
+    three = [
+        attend(
+            queries[2 * c : 2 * c + 2].reshape(B, HD),
+            r3[2 - 2 * c : 4 - 2 * c, 0].reshape(B, HD),
+            r3[2 - 2 * c : 4 - 2 * c, 1].reshape(B, HD),
+        )
+        for c in range(2)
+    ]
+    four = pool_halves(queries.astype(F32).reshape(2 * B, HD), 16)
+
+    def mix(apart):
+        return jnp.where((col == row) | (col == (row ^ apart)), 0.5, 0.0).astype(BF)
+
+    five = dot(mix(4), four).astype(BF)
+    six = dot(mix(2), five).astype(BF)
+
     relay_left.wait_recv()
     relay_right.wait_recv()
+    for b in (0, 5):
+        turn(core, b)
+        turn(1 - core, b)
 
     for store, w in ((k0, wk_s), (v0, wv)):
         for b in (0, 5):
@@ -228,53 +266,6 @@
         return carry
 
     lax.fori_loop(0, NEAR_FIRST, near, 0)
-
-    arrived(r3.at[pl.ds(0, 3)], 3)
-    five_rows, six_rows = pool_matrix(64, 4), pool_matrix(32, 2)
-    for i in range(2):
-        l4 = pool_halves(r3[:, i].astype(F32).reshape(2 * B, HD), 16)
-        l5 = dot(five_rows, l4).astype(BF)
-        s4[i] = l4
-        s5[i] = l5
-        s6[i] = dot(six_rows, l5).astype(BF)
-    for p in over6:
-        send(s6, r6.at[(me // 4) % 4], 6, (p, core))
-    for p in over5:
-        send(s5, r5.at[(me // 4) % 2], 5, (p, core))
-    send(s4, r4, 4, (mirror(me), core))
-
-    queries = r3[:, 2]
-    three = [
-        attend(
-            queries[2 * c : 2 * c + 2].reshape(B, HD),
-            r3[2 - 2 * c : 4 - 2 * c, 0].reshape(B, HD),
-            r3[2 - 2 * c : 4 - 2 * c, 1].reshape(B, HD),
-        )
-        for c in range(2)
-    ]
-    four = pool_halves(queries.astype(F32).reshape(2 * B, HD), 16)
-
-    def mix(apart):
-        return jnp.where((col == row) | (col == (row ^ apart)), 0.5, 0.0).astype(BF)
-
-    five = dot(mix(4), four).astype(BF)
-    six = dot(mix(2), five).astype(BF)
-
-    lax.fori_loop(NEAR_FIRST, heads, near, 0)
-
-    arrived(r2, 2)
-
-    def second(h, carry):
-        state = attend(q2[h], r2[h, 0], r2[h, 1])
-        for b in range(4):
-            rows = slice(b * B, (b + 1) * B)
-            part = tuple(twice(twice(x[b * 32 : (b + 1) * 32], 1), 1) for x in state)
-            peak, total, numer = merge((fpeak[h, rows], ftot[h, rows], fnum[h, rows]), part)
-            fnum[h, rows] = numer / total
-            fpeak[h, rows] = peak + jnp.log2(total)
-        return carry
-
-    lax.fori_loop(0, heads, second, 0)
 
     arrived(r6, 6)
     state = attend(six, r6[:, 0].reshape(B, HD), r6[:, 1].reshape(B, HD))
@@ -297,6 +288,21 @@
     for p in mates:
         send(sr.at[p % 4], rr.at[my_head], 10, (p, core))
     rr[my_head] = sr[place4]
+    lax.fori_loop(NEAR_FIRST, heads, near, 0)
+    arrived(r2, 2)
+
+    def second(h, carry):
+        state = attend(q2[h], r2[h, 0], r2[h, 1])
+        for b in range(4):
+            rows = slice(b * B, (b + 1) * B)
+            part = tuple(twice(twice(x[b * 32 : (b + 1) * 32], 1), 1) for x in state)
+            peak, total, numer = merge((fpeak[h, rows], ftot[h, rows], fnum[h, rows]), part)
+            fnum[h, rows] = numer / total
+            fpeak[h, rows] = peak + jnp.log2(total)
+        return carry
+
+    lax.fori_loop(0, heads, second, 0, unroll=True)
+
     arrived(rr.at[pl.ds(0, 3)], 10)
 
     own = col[:64] == (place4 % 2) * 64 + row[:64]
@@ -317,7 +323,7 @@
             out_ref[rows, cols] = dot(perm, mixed.astype(BF)).astype(BF)
         return carry
 
-    lax.fori_loop(0, heads, last, 0)
+    lax.fori_loop(0, heads, last, 0, unroll=True)
 
     to_right.wait_send()
     to_left.wait_send()
@@ -341,7 +347,7 @@
 
     width = heads * HD
     scratch = [
-        vm(rows, feats), vm(2, 6, B, feats), vm(2 * feats, 2, width), vm(2 * feats, width),
+        vm(2, rows + 2 * B, feats), vm(2, 6, B, feats), vm(2 * feats, 2, width), vm(2 * feats, width),
         vm(2 * feats, width), vm(2 * feats, width), vm(3, rows, width, dtype=F32),
         vm(heads, rows, HD), vm(heads, rows + 2 * B, HD), vm(heads, rows + 2 * B, HD),
         vm(heads, 256, HD), vm(heads, 256, HD), vm(heads, 256, HD), vm(heads, 128, HD),

time: 35.8 us -> 32.7 us (0.913); the launches traced: 35.7 us -> 32.2 us
  Pallas kernels: 34.2 us -> 30.7 us
    pallas_call x1, Pallas kernels: 34.2 us -> 30.7 us  [on_device(): pl.pallas_call(functools.partial(kernel, count), out_shape=jax.ShapeDtype...]
where the time goes in v3:
time: 32.7 us; the launch traced here: 32.2 us
  Pallas kernels  30.7 us (94%)
  local copies, waits for them, and re-layouts  0.8 us (2%)
  other arithmetic  0.68 us (2%)
    pallas_call x1, Pallas kernels, on_device(): pl.pallas_call(functools.partial(kernel, count), out_shape=jax.ShapeDtype...  30.7 us
    unnamed x1, local copies, waits for them, and re-layouts  0.8 us
    another operation x1, other arithmetic, on_device(): jnp.stack([span_start, span_end])  0.68 us

profile of v3, /device:TPU:1, one launch (start us, length us, event | category | flops | bytes accessed | tf_op | source)
XLA Modules:
  0.0 32.2 jit_solution(5075861617525389525)
XLA Ops:
  0.0 0.7 %pad_add_fusion.span_hbm = s32[2,4]{1,0:T(2,128)S(1)} fusion(s32[1,4]{1,0:T(1,128)} %bitcast.2, s32[1,4]{1,0:T(1,128)} %bitcast.3), kind=kLoop, calls=%fused_computation | loop fusion | flops 8 | bytes 64 | tf_op jit(solution)/shard_map/stack | solution.py:373
  0.7 30.7 %htransformer.1 = bf16[512,512]{1,0:T(8,128)(2,1)S(1)} custom-call(bf16[512,512]{1,0:T(8,128)(2,1)} %tok_hbm.1, bf16[1024,2,512]{2,1,0:T(2,128)(2,1)} %wqk_hbm.1, bf16[1024,512]{1,0:T(8,128)(2,1)} %wv_hbm.1, s32[2,4]{1,0:T(2,128)S(1)} %pad_add_fusion.span_hbm), custom_call_target="tpu_custom_call" | custom-call | flops 3000000000 | bytes 5000000 | tf_op jit(solution)/shard_map/htransformer/pallas_call | solution.py:362
  31.4 0.8 %copy.7 = bf16[512,512]{1,0:T(8,128)(2,1)} copy(bf16[512,512]{1,0:T(8,128)(2,1)S(1)} %htransformer.1) | data formatting | bytes 1048576

commit v4 on v3

--- a/solution.py
+++ b/solution.py
@@ -70,8 +70,8 @@
     out_ref,
     raw, tokp, wqk, wv, wq_s, wk_s, acc,
     q0, k0, v0, q1, k1, v1, q2,
-    s2, s3, s4, s5, s6, sr,
-    r2, r3, r4, r5, r6, rr,
+    s2, s3, sq, s4, s5, s6, sr,
+    r2, r3, rq, r4, r5, r6, rr,
     fpeak, ftot, fnum,
     span, load_sem, send_sem, recv_sem,
 ):
@@ -163,6 +163,7 @@
         turn(1 - core, b)
     theirs = tokp[1 - core, 1:5].reshape(4 * B, 512)
 
+    my_head = head_of(me)
     for i in range(3):
         full = (acc[i] + dot(theirs, weights[i][pl.ds(other, 512), :])).astype(BF)
         l1 = pool_halves(full.astype(F32), 4)
@@ -170,21 +171,57 @@
         l3 = pool_halves(l2.astype(F32), 4)
         for h in range(heads):
             cols = slice(h * HD, (h + 1) * HD)
-            s3[h, i] = l3[:, cols]
             if i < 2:
+                s3[h, i] = l3[:, cols]
                 (k0, v0)[i][h, B : 5 * B] = full[:, cols]
                 (k1, v1)[i][h] = l1[:, cols]
                 s2[h, i] = l2[:, cols]
             else:
+                sq[h] = l3[:, cols]
                 q0[h] = full[:, cols]
                 q1[h] = l1[:, cols]
                 q2[h] = l2[:, cols]
-
-    my_head = head_of(me)
-    for p in mates:
-        send(s3.at[head_of(p)], r3.at[place4], 3, (p, core))
+        if i == 1:
+            for p in mates:
+                send(s3.at[head_of(p)], r3.at[place4], 3, (p, core))
+        if i == 2:
+            for p in mates:
+                send(sq.at[head_of(p)], rq.at[place4], 11, (p, core))
     send(s2, r2, 2, (flip(me, 1), core))
     r3[place4] = s3[my_head]
+    rq[place4] = sq[my_head]
+
+    turned = reversed_bits(lax.broadcasted_iota(jnp.int32, (1, B), 1))
+    none = jnp.zeros((1, B), F32)
+    loads[3].wait()
+    biases = []
+    for b in range(4):
+        before = (me * 4 + b - 1) * B + turned
+        after = (me * 4 + b + 1) * B + turned
+        biases.append(
+            jnp.concatenate(
+                [
+                    jnp.where(before >= span[0, b], 0.0, -jnp.inf),
+                    none,
+                    jnp.where(after < span[1, b], 0.0, -jnp.inf),
+                ],
+                axis=1,
+            )
+        )
+
+    def near(blocks, h, carry):
+        for b in blocks:
+            c = b // 2
+            o = (c ^ 1) * B
+            rows = slice(b * B, (b + 1) * B)
+            fine = attend(q0[h, rows], k0[h, b * B : (b + 3) * B], v0[h, b * B : (b + 3) * B], biases[b])
+            coarse = attend(q1[h, b * 64 : (b + 1) * 64], k1[h, o : o + B], v1[h, o : o + B])
+            state = merge(fine, tuple(twice(x, 1) for x in coarse))
+            fpeak[h, rows], ftot[h, rows], fnum[h, rows] = state
+        return carry
+
+    inner, outer = functools.partial(near, (1, 2)), functools.partial(near, (0, 3))
+    lax.fori_loop(0, heads, inner, 0)
 
     to_right.wait_recv()
     relay_left = send(raw.at[core, pl.ds(0, B)], raw.at[core, pl.ds(0, B)], 8, twin)
@@ -204,7 +241,8 @@
         send(s5, r5.at[(me // 4) % 2], 5, (p, core))
     send(s4, r4, 4, (mirror(me), core))
 
-    queries = r3[:, 2]
+    arrived(rq.at[pl.ds(0, 3)], 11)
+    queries = rq[...]
     three = [
         attend(
             queries[2 * c : 2 * c + 2].reshape(B, HD),
@@ -236,36 +274,7 @@
             for h in range(heads):
                 store[h, b * B : (b + 1) * B] = full[:, h * HD : (h + 1) * HD]
 
-    turned = reversed_bits(lax.broadcasted_iota(jnp.int32, (1, B), 1))
-    none = jnp.zeros((1, B), F32)
-    loads[3].wait()
-    biases = []
-    for b in range(4):
-        before = (me * 4 + b - 1) * B + turned
-        after = (me * 4 + b + 1) * B + turned
-        biases.append(
-            jnp.concatenate(
-                [
-                    jnp.where(before >= span[0, b], 0.0, -jnp.inf),
-                    none,
-                    jnp.where(after < span[1, b], 0.0, -jnp.inf),
-                ],
-                axis=1,
-            )
-        )
-
-    def near(h, carry):
-        for b in range(4):
-            c = b // 2
-            o = (c ^ 1) * B
-            rows = slice(b * B, (b + 1) * B)
-            fine = attend(q0[h, rows], k0[h, b * B : (b + 3) * B], v0[h, b * B : (b + 3) * B], biases[b])
-            coarse = attend(q1[h, b * 64 : (b + 1) * 64], k1[h, o : o + B], v1[h, o : o + B])
-            state = merge(fine, tuple(twice(x, 1) for x in coarse))
-            fpeak[h, rows], ftot[h, rows], fnum[h, rows] = state
-        return carry
-
-    lax.fori_loop(0, NEAR_FIRST, near, 0)
+    lax.fori_loop(0, NEAR_FIRST, outer, 0)
 
     arrived(r6, 6)
     state = attend(six, r6[:, 0].reshape(B, HD), r6[:, 1].reshape(B, HD))
@@ -280,15 +289,21 @@
         result = numer / total
         level = peak + jnp.log2(total)
         lines.append(jnp.sum(jnp.where(row == col, level, 0.0), axis=0, keepdims=True))
-        sr[2 * c, :64] = result[:64]
-        sr[2 * c + 1, :64] = result[64:]
-    stats = jnp.where(row[:8] == 0, lines[0], lines[1])
+        sr[2 * c, :64] = result[:64].astype(BF)
+        sr[2 * c + 1, :64] = result[64:].astype(BF)
+    rest = jnp.where(row[:16] < 8, lines[0], lines[1])
+    stats = jnp.zeros((16, HD), F32)
+    for k in range(3):
+        piece = rest.astype(BF).astype(F32)
+        stats = jnp.where(row[:16] % 8 == k, piece, stats)
+        rest = rest - piece
+    stats = stats.astype(BF)
     for j in range(4):
         sr[j, 64:] = stats
     for p in mates:
         send(sr.at[p % 4], rr.at[my_head], 10, (p, core))
     rr[my_head] = sr[place4]
-    lax.fori_loop(NEAR_FIRST, heads, near, 0)
+    lax.fori_loop(NEAR_FIRST, heads, outer, 0)
     arrived(r2, 2)
 
     def second(h, carry):
@@ -308,13 +323,14 @@
     own = col[:64] == (place4 % 2) * 64 + row[:64]
 
     def last(h, carry):
-        line = rr[h, pl.ds(64 + place4 // 2, 1)]
+        pieces = rr[h, 64:].astype(F32)
+        line = jnp.sum(jnp.where(row[:16] // 8 == place4 // 2, pieces, 0.0), axis=0, keepdims=True)
         level = jnp.sum(jnp.where(own, line, 0.0), axis=1, keepdims=True)
         level = jnp.broadcast_to(level, (64, HD))
         cols = pl.ds(pl.multiple_of(h * HD, HD), HD)
         for b in range(4):
             rows = slice(b * B, (b + 1) * B)
-            far, far_level = rr[h, b * 16 : (b + 1) * 16], level[b * 16 : (b + 1) * 16]
+            far, far_level = rr[h, b * 16 : (b + 1) * 16].astype(F32), level[b * 16 : (b + 1) * 16]
             for _ in range(3):
                 far, far_level = twice(far, 1), twice(far_level, 1)
             close = fnum[h, rows]
@@ -331,6 +347,7 @@
     relay_right.wait_send()
     gone(r2, 2)
     gone(r3.at[pl.ds(0, 3)], 3)
+    gone(rq.at[pl.ds(0, 3)], 11)
     gone(r4, 4)
     gone(r5, 5)
     gone(r6, 6)
@@ -351,13 +368,13 @@
         vm(2 * feats, width), vm(2 * feats, width), vm(3, rows, width, dtype=F32),
         vm(heads, rows, HD), vm(heads, rows + 2 * B, HD), vm(heads, rows + 2 * B, HD),
         vm(heads, 256, HD), vm(heads, 256, HD), vm(heads, 256, HD), vm(heads, 128, HD),
-        vm(heads, 2, 128, HD), vm(heads, 3, 64, HD), vm(2, 128, HD), vm(2, 64, HD), vm(2, 32, HD),
-        vm(4, 72, HD, dtype=F32),
-        vm(heads, 2, 128, HD), vm(4, 3, 64, HD), vm(2, 128, HD), vm(2, 2, 64, HD), vm(4, 2, 32, HD),
-        vm(heads, 72, HD, dtype=F32),
+        vm(heads, 2, 128, HD), vm(heads, 2, 64, HD), vm(heads, 64, HD), vm(2, 128, HD), vm(2, 64, HD), vm(2, 32, HD),
+        vm(4, 80, HD),
+        vm(heads, 2, 128, HD), vm(4, 2, 64, HD), vm(4, 64, HD), vm(2, 128, HD), vm(2, 2, 64, HD), vm(4, 2, 32, HD),
+        vm(heads, 80, HD),
         vm(heads, rows, HD, dtype=F32), vm(heads, rows, HD, dtype=F32), vm(heads, rows, HD, dtype=F32),
         pltpu.SMEM((2, 4), jnp.int32),
-        pltpu.SemaphoreType.DMA((4,)), pltpu.SemaphoreType.DMA((11,)), pltpu.SemaphoreType.DMA((11,)),
+        pltpu.SemaphoreType.DMA((4,)), pltpu.SemaphoreType.DMA((12,)), pltpu.SemaphoreType.DMA((12,)),
     ]
     return pl.pallas_call(
         functools.partial(kernel, count),

time: 32.7 us -> 31.8 us (0.972)
  Pallas kernels: 30.7 us -> 30 us
    pallas_call x1, Pallas kernels: 30.7 us -> 30 us  [on_device(): pl.pallas_call(functools.partial(kernel, count), out_shape=jax.ShapeDtype...]
where the time goes in v4:
time: 31.8 us; the launch traced here: 31.5 us
  Pallas kernels  30 us (94%)
  local copies, waits for them, and re-layouts  0.8 us (3%)
  other arithmetic  0.68 us (2%)
    pallas_call x1, Pallas kernels, on_device(): pl.pallas_call(functools.partial(kernel, count), out_shape=jax.ShapeDtype...  30 us
    unnamed x1, local copies, waits for them, and re-layouts  0.8 us
    another operation x1, other arithmetic, on_device(): jnp.stack([span_start, span_end])  0.68 us

profile of v4, /device:TPU:1, one launch (start us, length us, event | category | flops | bytes accessed | tf_op | source)
XLA Modules:
  0.0 31.5 jit_solution(4425468072647407819)
XLA Ops:
  0.0 0.7 %pad_add_fusion.span_hbm = s32[2,4]{1,0:T(2,128)S(1)} fusion(s32[1,4]{1,0:T(1,128)} %bitcast.2, s32[1,4]{1,0:T(1,128)} %bitcast.3), kind=kLoop, calls=%fused_computation | loop fusion | flops 8 | bytes 64 | tf_op jit(solution)/shard_map/stack | solution.py:390
  0.7 30.0 %htransformer.1 = bf16[512,512]{1,0:T(8,128)(2,1)S(1)} custom-call(bf16[512,512]{1,0:T(8,128)(2,1)} %tok_hbm.1, bf16[1024,2,512]{2,1,0:T(2,128)(2,1)} %wqk_hbm.1, bf16[1024,512]{1,0:T(8,128)(2,1)} %wv_hbm.1, s32[2,4]{1,0:T(2,128)S(1)} %pad_add_fusion.span_hbm), custom_call_target="tpu_custom_call" | custom-call | flops 3000000000 | bytes 5000000 | tf_op jit(solution)/shard_map/htransformer/pallas_call | solution.py:379
  30.7 0.8 %copy.7 = bf16[512,512]{1,0:T(8,128)(2,1)} copy(bf16[512,512]{1,0:T(8,128)(2,1)S(1)} %htransformer.1) | data formatting | bytes 1048576

commit v5 on v4

--- a/solution.py
+++ b/solution.py
@@ -68,7 +68,7 @@
     count,
     tok_hbm, wqk_hbm, wv_hbm, span_hbm,
     out_ref,
-    raw, tokp, wqk, wv, wq_s, wk_s, acc,
+    tok_raw, tokp, wqk, wv, wq_s, wk_s, acc,
     q0, k0, v0, q1, k1, v1, q2,
     s2, s3, sq, s4, s5, s6, sr,
     r2, r3, rq, r4, r5, r6, rr,
@@ -76,10 +76,10 @@
     span, load_sem, send_sem, recv_sem,
 ):
     me, core = lax.axis_index("seq"), lax.axis_index("head")
-    heads, rows = q0.shape[0], q0.shape[1]
+    heads = q0.shape[0]
 
     loads = [
-        pltpu.make_async_copy(tok_hbm, raw.at[core, pl.ds(B, rows)], load_sem.at[0]),
+        pltpu.make_async_copy(tok_hbm, tok_raw, load_sem.at[0]),
         pltpu.make_async_copy(wqk_hbm, wqk, load_sem.at[1]),
         pltpu.make_async_copy(wv_hbm, wv, load_sem.at[2]),
         pltpu.make_async_copy(span_hbm, span, load_sem.at[3]),
@@ -113,6 +113,10 @@
     col = lax.broadcasted_iota(jnp.int32, (B, B), 1)
     perm = jnp.where(reversed_bits(row) == col, 1.0, 0.0).astype(BF)
 
+    loads[0].wait()
+    for b in range(4):
+        tokp[core, b + 1] = dot(perm, tok_raw[b * B : (b + 1) * B]).astype(BF)
+
     pl.semaphore_wait(barrier, len(greet))
 
     def send(src, dst, sem, device):
@@ -129,16 +133,10 @@
     def gone(ref, sem):
         pltpu.make_async_copy(ref, ref, send_sem.at[sem]).wait()
 
-    swap = send(tok_hbm, raw.at[core, pl.ds(B, rows)], 0, twin)
-    to_right = send(tok_hbm.at[pl.ds(rows - B, B)], raw.at[core, pl.ds(0, B)], 1, (right, core))
-    to_left = send(tok_hbm.at[pl.ds(0, B)], raw.at[core, pl.ds(rows + B, B)], 7, (left, core))
-
-    def turn(side, b):
-        tokp[side, b] = dot(perm, raw[side, b * B : (b + 1) * B]).astype(BF)
-
-    loads[0].wait()
-    for b in range(1, 5):
-        turn(core, b)
+    swap = send(tokp.at[core, pl.ds(1, 4)], tokp.at[core, pl.ds(1, 4)], 0, twin)
+    to_right = send(tokp.at[core, 4], tokp.at[core, 0], 1, (right, core))
+    to_left = send(tokp.at[core, 1], tokp.at[core, 5], 7, (left, core))
+
     loads[1].wait()
 
     def split(i, carry):
@@ -159,8 +157,6 @@
         acc[i] = dot(mine, w[pl.ds(half, 512), :])
 
     swap.wait()
-    for b in range(1, 5):
-        turn(1 - core, b)
     theirs = tokp[1 - core, 1:5].reshape(4 * B, 512)
 
     my_head = head_of(me)
@@ -224,9 +220,9 @@
     lax.fori_loop(0, heads, inner, 0)
 
     to_right.wait_recv()
-    relay_left = send(raw.at[core, pl.ds(0, B)], raw.at[core, pl.ds(0, B)], 8, twin)
+    relay_left = send(tokp.at[core, 0], tokp.at[core, 0], 8, twin)
     to_left.wait_recv()
-    relay_right = send(raw.at[core, pl.ds(rows + B, B)], raw.at[core, pl.ds(rows + B, B)], 9, twin)
+    relay_right = send(tokp.at[core, 5], tokp.at[core, 5], 9, twin)
     arrived(r3.at[pl.ds(0, 3)], 3)
     five_rows, six_rows = pool_matrix(64, 4), pool_matrix(32, 2)
     for i in range(2):
@@ -261,10 +257,6 @@
 
     relay_left.wait_recv()
     relay_right.wait_recv()
-    for b in (0, 5):
-        turn(core, b)
-        turn(1 - core, b)
-
     for store, w in ((k0, wk_s), (v0, wv)):
         for b in (0, 5):
             full = dot(tokp[core, b], w[pl.ds(half, 512), :]) + dot(
@@ -364,7 +356,7 @@
 
     width = heads * HD
     scratch = [
-        vm(2, rows + 2 * B, feats), vm(2, 6, B, feats), vm(2 * feats, 2, width), vm(2 * feats, width),
+        vm(rows, feats), vm(2, 6, B, feats), vm(2 * feats, 2, width), vm(2 * feats, width),
         vm(2 * feats, width), vm(2 * feats, width), vm(3, rows, width, dtype=F32),
         vm(heads, rows, HD), vm(heads, rows + 2 * B, HD), vm(heads, rows + 2 * B, HD),
         vm(heads, 256, HD), vm(heads, 256, HD), vm(heads, 256, HD), vm(heads, 128, HD),

time: 31.8 us -> 31.4 us (0.987)
  no operation moved by 1% of the time
where the time goes in v5:
time: 31.4 us; the launch traced here: 31.3 us
  Pallas kernels  29.8 us (95%)
  local copies, waits for them, and re-layouts  0.8 us (3%)
  other arithmetic  0.68 us (2%)
    pallas_call x1, Pallas kernels, on_device(): pl.pallas_call(functools.partial(kernel, count), out_shape=jax.ShapeDtype...  29.8 us
    unnamed x1, local copies, waits for them, and re-layouts  0.8 us
    another operation x1, other arithmetic, on_device(): jnp.stack([span_start, span_end])  0.68 us

profile of v5, /device:TPU:1, one launch (start us, length us, event | category | flops | bytes accessed | tf_op | source)
XLA Modules:
  0.0 31.3 jit_solution(7557203052775675751)
XLA Ops:
  0.0 0.7 %pad_add_fusion.span_hbm = s32[2,4]{1,0:T(2,128)S(1)} fusion(s32[1,4]{1,0:T(1,128)} %bitcast.2, s32[1,4]{1,0:T(1,128)} %bitcast.3), kind=kLoop, calls=%fused_computation | loop fusion | flops 8 | bytes 64 | tf_op jit(solution)/shard_map/stack | solution.py:382
  0.7 29.8 %htransformer.1 = bf16[512,512]{1,0:T(8,128)(2,1)S(1)} custom-call(bf16[512,512]{1,0:T(8,128)(2,1)} %tok_hbm.1, bf16[1024,2,512]{2,1,0:T(2,128)(2,1)} %wqk_hbm.1, bf16[1024,512]{1,0:T(8,128)(2,1)} %wv_hbm.1, s32[2,4]{1,0:T(2,128)S(1)} %pad_add_fusion.span_hbm), custom_call_target="tpu_custom_call" | custom-call | flops 3000000000 | bytes 5000000 | tf_op jit(solution)/shard_map/htransformer/pallas_call | solution.py:371
  30.5 0.8 %copy.7 = bf16[512,512]{1,0:T(8,128)(2,1)} copy(bf16[512,512]{1,0:T(8,128)(2,1)S(1)} %htransformer.1) | data formatting | bytes 1048576
